TPU v7x, 512 devices: a whole 4x4x16 slice. The times are simulated.
512 devices in a mesh: tensor: 16 (over x, z_hi), feature: 8 (over y, core), dp: 4 (over z_lo).
Axes of the slice: x: 4, y: 4, z: 16 (z_hi: 4, z_lo: 4; z = z_hi * 4 + z_lo), core: 2. Of those that a mesh axis runs over, the one named last changes fastest.
Arguments:
- mlp_input: bfloat16 [64, 4096], P(None, ('feature', 'dp')), may hold values from -6 to 6
- gate_weight: bfloat16 [4096, 28672], P(('feature', 'dp'), 'tensor'), may hold values from -0.09375 to 0.09375
- up_weight: bfloat16 [4096, 28672], P(('feature', 'dp'), 'tensor'), may hold values from -0.09375 to 0.09375
- down_weight: bfloat16 [28672, 4096], P('tensor', ('feature', 'dp')), may hold values from -0.03125 to 0.03125
- down_encoder: bfloat16 [65536, 4096], P('tensor', ('feature', 'dp')), may hold values from -6 to 6
- feature_ids: int32 [32], replicated, may hold values from 0 to 65535
- up_decoder: bfloat16 [131072, 4096], P('tensor', ('feature', 'dp')), may hold values from -0.09375 to 0.09375
- latent_ids: int32 [64, 64], replicated, may hold values from 0 to 131071, as said below
- latent_acts: float32 [64, 64], P('dp', 'tensor'), may hold values from 0.5 to 4
Outputs:
- attribution: float32 [32, 64, 64], P('feature', 'dp', 'tensor')
Inputs may be any that keep to these rules, and one draw needn't show every extreme that they name: `latent_ids`: the 64 latents of one token are distinct.
All inputs are finite; a program needn't handle non-finite values.
Results may differ from a plain program's by a relative error of at most 0.0029.
Values may be sent and summed in bfloat16 or wider, within the bound.
No kernel may reach another device: no remote copies, remote signals or barrier semaphores. Data moves between devices by JAX's collectives and lax.ppermute only.
A program may use at most 64 MiB of HBM per device.

v0:
```python
import math
import jax
import jax.numpy as jnp
from jax import lax
from jax.sharding import PartitionSpec as P


def factors(gate_pre, up_pre):
    sigmoid_gate = jax.nn.sigmoid(gate_pre)
    gate_factor = up_pre * sigmoid_gate * (1.0 + gate_pre * (1.0 - sigmoid_gate))
    up_factor = gate_pre * sigmoid_gate
    return (gate_factor, up_factor)


def arrange_blocks(partial_value, count_tensor, count_feature, count_data):
    features = partial_value.shape[0]
    tokens = partial_value.shape[1]
    slots = partial_value.shape[2]
    arranged = partial_value.reshape(
        count_feature,
        features // count_feature,
        count_data,
        tokens // count_data,
        count_tensor,
        slots // count_tensor,
    )
    arranged = arranged.transpose(4, 0, 2, 1, 3, 5)
    return arranged.reshape(
        count_tensor * count_feature * count_data,
        features // count_feature,
        tokens // count_data,
        slots // count_tensor,
    )


def on_device(
    mlp_input,
    gate_weight,
    up_weight,
    down_weight,
    down_encoder,
    feature_ids,
    up_decoder,
    latent_ids,
    latent_acts,
):
    contract = (((1,), (1,)), ((), ()))
    tensor_rank = lax.axis_index("tensor")
    tokens = mlp_input.shape[0]
    dblk = gate_weight.shape[0]
    ffblk = gate_weight.shape[1]
    features = feature_ids.shape[0]
    count_tensor = lax.axis_size("tensor")
    count_feature = lax.axis_size("feature")
    count_data = lax.axis_size("dp")
    enc_rows = down_encoder.shape[0]
    local_ids = feature_ids - tensor_rank * enc_rows
    picker = (local_ids[:, None] == jnp.arange(enc_rows, dtype=jnp.int32)[None, :]).astype(
        jnp.bfloat16
    )
    chosen = lax.psum(jnp.dot(picker, down_encoder, preferred_element_type=jnp.float32), "tensor")
    cotangent = chosen.astype(jnp.bfloat16)
    neuron_part = lax.dot_general(
        cotangent, down_weight, contract, preferred_element_type=jnp.float32
    )
    gate_part = jnp.dot(mlp_input, gate_weight, preferred_element_type=jnp.float32)
    up_part = jnp.dot(mlp_input, up_weight, preferred_element_type=jnp.float32)
    gate_pre, up_pre, neuron_grad = lax.psum((gate_part, up_part, neuron_part), ("feature", "dp"))
    gate_factor, up_factor = factors(gate_pre, up_pre)
    per_block = math.gcd(features, 8)
    grouped_rows = neuron_grad.reshape(features // per_block, per_block, ffblk)

    def feature_block(grad_rows):
        grad_gate = (
            (grad_rows[:, None, :] * gate_factor[None])
            .astype(jnp.bfloat16)
            .reshape(per_block * tokens, ffblk)
        )
        grad_up = (
            (grad_rows[:, None, :] * up_factor[None])
            .astype(jnp.bfloat16)
            .reshape(per_block * tokens, ffblk)
        )
        width_grad = lax.dot_general(
            grad_gate, gate_weight, contract, preferred_element_type=jnp.float32
        )
        width_grad = width_grad + lax.dot_general(
            grad_up, up_weight, contract, preferred_element_type=jnp.float32
        )
        return width_grad.reshape(per_block, tokens, dblk)

    width_part = lax.map(feature_block, grouped_rows).reshape(features, tokens, dblk)
    dec_rows = up_decoder.shape[0]
    local_latents = latent_ids - tensor_rank * dec_rows
    owner_mask = jnp.logical_and(local_latents >= 0, local_latents < dec_rows)
    picked = jnp.take(up_decoder, jnp.clip(local_latents, 0, dec_rows - 1), axis=0)
    picked = picked * owner_mask[:, :, None].astype(jnp.bfloat16)
    width_full = lax.psum(width_part, "tensor")
    partial_value = jnp.einsum(
        "ftd,tkd->ftk", width_full, picked.astype(jnp.float32), precision=lax.Precision.HIGHEST
    )
    arranged = arrange_blocks(partial_value, count_tensor, count_feature, count_data)
    own_block = lax.psum_scatter(
        arranged, ("tensor", "feature", "dp"), scatter_dimension=0, tiled=True
    )[0]
    return own_block * latent_acts[None, :, :]


def solution(mesh):
    in_specs = (
        P(None, ("feature", "dp")),
        P(("feature", "dp"), "tensor"),
        P(("feature", "dp"), "tensor"),
        P("tensor", ("feature", "dp")),
        P("tensor", ("feature", "dp")),
        P(),
        P("tensor", ("feature", "dp")),
        P(),
        P("dp", "tensor"),
    )
    out_specs = P("feature", "dp", "tensor")
    return jax.shard_map(
        on_device, mesh=mesh, in_specs=in_specs, out_specs=out_specs, check_vma=False
    )
```

profile of v0, /device:TPU:2, one launch (start us, length us, event | category | flops | bytes accessed | tf_op | source)
XLA Modules:
  0.0 1137.1 jit_solution(10292003025647488974)
XLA Ops:
  7.4 1.6 fusion.5
  9.0 99.8 %psum.35 = bf16[32,128]{1,0:T(8,128)(2,1)S(1)} all-reduce(f32[32,128]{1,0:T(8,128)S(1)} %fusion.5), channel_id=1, replica_groups=mesh['tensor'=16,'feature'=8,'dp'=4] {'tensor'}, use_global_device_ids=true, to_apply=%region_0.0 | all-reduce | flops 4096 | bytes 24576 | tf_op jit(solution)/shard_map/psum | solution.py:61
  108.8 2.0 fusion.12
  110.8 1.7 fusion.13
  112.5 1.0 convolution_bitcast_fusion
  113.5 283.3 %all-reduce.10.cloned.1.call-done = (f32[4,8,1792]{2,1,0:T(8,128)}, f32[64,1792]{1,0:T(8,128)}, f32[64,1792]{1,0:T(8,128)}) async-done(((f32[4,8,1792]{2,1,0:T(8,128)}, f32[64,1792]{1,0:T(8,128)}, f32[64,1792]{1,0:T(8,128)}), (f32[4,8,1792]{2,1,0:T(8,128)}, f32[64,1792]{1,0:T(8,128)}, f32[64,1792]{1,0:T(8,128)})) %all-reduce.10.cloned.1.call-update) | async-done | bytes 1146896 | tf_op jit(solution)/shard_map/psum | solution.py:68
  396.9 1.4 fusion.6
  398.2 16.5 %while.10 = (s32[]{:T(128)}, f32[4,8,64,128]{3,1,0,2:T(8,128)}, f32[4,8,1792]{2,1,0:T(8,128)}, f32[64,1792]{1,0:T(8,128)S(1)}, bf16[128,1792]{1,0:T(8,128)(2,1)S...) while((s32[]{:T(128)}, f32[4,8,64,128]{3,1,0,2:T(8,128)}, f32[4,8,1792]{2,1,0:T(8,128)}, ...), condition=%wide.region_5.6_spmd, body=%wide.region_4.5_spmd.sunk | while | flops 473497600 | bytes 12493429 | solution.py:92
  398.3 0.8 dynamic-slice_bitcast_fusion.3
  401.5 0.9 copy_dynamic-update-slice_fusion.2
  405.6 0.9 copy_dynamic-update-slice_fusion.2
  406.5 0.8 dynamic-slice_bitcast_fusion.3
  409.7 0.9 copy_dynamic-update-slice_fusion.2
  410.6 0.8 dynamic-slice_bitcast_fusion.3
  413.9 0.9 copy_dynamic-update-slice_fusion.2
  415.0 12.1 %gather_fusion = bf16[4096,128]{1,0:T(8,128)(2,1)S(1)} fusion(bf16[8192,128]{1,0:T(8,128)(2,1)S(1)} %copy-done, s32[4096]{0:T(1024)S(1)} %broadcast_clamp_fusion), kind=kCustom, calls=%fused_computation | custom fusion | bytes 2113536 | tf_op jit(solution)/shard_map/jit(_take)/gather | solution.py:96
  427.1 197.9 %all-reduce.6.cloned.1.call-done = f32[32,64,128]{2,0,1:T(8,128)} async-done(((f32[32,64,128]{2,0,1:T(8,128)}), f32[32,64,128]{2,0,1:T(8,128)}) %all-reduce.6.cloned.1.call-update) | async-done | bytes 1048592 | tf_op jit(solution)/shard_map/psum | solution.py:98
  625.0 4.4 convolution_bitcast_fusion.1
  629.3 1.8 copy.18
  631.1 3.2 reshape.39
  634.3 3.4 copy.19
  637.7 4.7 copy.20
  642.4 486.8 %all-reduce.8.cloned.1.call-done = f32[512,4,16,4]{2,3,1,0:T(4,128)} async-done(((f32[512,4,16,4]{2,3,1,0:T(4,128)}), f32[512,4,16,4]{2,3,1,0:T(4,128)}) %all-reduce.8.cloned.1.call-update) | async-done | bytes 524304
  1129.2 1.3 fusion.8
  (42 shorter events, 11.4 us)
Async XLA Ops:
  6.5 408.4 %copy-start = (bf16[8192,128]{1,0:T(8,128)(2,1)S(1)}, bf16[8192,128]{1,0:T(8,128)(2,1)}, u32[]{:S(2)}) copy-start(bf16[8192,128]{1,0:T(8,128)(2,1)} %param.17) | copy-start | bytes 6291460
  6.5 104.3 %copy-start.1 = (bf16[128,1792]{1,0:T(8,128)(2,1)S(1)}, bf16[128,1792]{1,0:T(8,128)(2,1)}, u32[]{:S(2)}) copy-start(bf16[128,1792]{1,0:T(8,128)(2,1)} %param.12) | copy-start | bytes 1376260
  6.5 106.0 %copy-start.3 = (bf16[1792,128]{1,0:T(8,128)(2,1)S(1)}, bf16[1792,128]{1,0:T(8,128)(2,1)}, u32[]{:S(2)}) copy-start(bf16[1792,128]{1,0:T(8,128)(2,1)} %param.14) | copy-start | bytes 1376260
  6.5 390.3 %all-reduce.10.cloned.1.call-start = ((), (), s32[]{:S(2)}) async-start(), calls=%async_computation.2 | async-start | bytes 2293760 | tf_op jit(solution)/shard_map/psum | solution.py:68
  113.5 511.5 %all-reduce.6.cloned.1.call-start = ((), (), s32[]{:S(2)}) async-start(), calls=%async_computation | async-start | bytes 2097152 | tf_op jit(solution)/shard_map/psum | solution.py:98
  398.2 16.6 %copy-start.4 = (s32[64,64]{1,0:T(8,128)S(1)}, s32[64,64]{1,0:T(8,128)}, u32[]{:S(2)}) copy-start(s32[64,64]{1,0:T(8,128)} %param.18) | copy-start | bytes 49156
  399.8 1.0 copy-start.2
  403.9 1.0 copy-start.2
  408.0 1.0 copy-start.2
  412.2 1.0 copy-start.2
  414.8 714.4 %all-reduce.8.cloned.1.call-start = ((), (), s32[]{:S(2)}) async-start(), calls=%async_computation.1 | async-start | bytes 8388608
  642.4 486.9 %copy-start.5 = (f32[16,4]{0,1:T(4,128)S(1)}, f32[16,4]{0,1:T(4,128)}, u32[]{:S(2)}) copy-start(f32[16,4]{0,1:T(4,128)} %param.19) | copy-start | bytes 772
Sparse Core Ops, SparseCore 0:
  113.6 283.2 all-reduce.9
  414.9 210.0 all-reduce.5
  642.5 486.6 all-reduce.7
where the time goes:
time: 1140 us
  waiting for transfers between devices  968 us (85%)
  blocking collectives  99.8 us (9%)
  local copies, waits for them, and re-layouts  33.6 us (3%)
  matrix products  15.8 us (1%)
  between operations  13.2 us (1%)
    unnamed x4, waiting for transfers between devices  487 us
    psum x1, waiting for transfers between devices, on_device(): lax.psum((gate_part, up_part, neuron_part), ('feature', 'dp'))  283 us
    psum x1, waiting for transfers between devices, on_device(): width_full = lax.psum(width_part, 'tensor')  198 us
    psum x1, blocking collectives, on_device(): lax.psum(jnp.dot(picker, down_encoder, preferred_element_type=jnp.float32...  99.8 us
  transfers between devices with their start and end apart: 3, of which 3 were waited for; matrix products, arithmetic and copies ran while one was open for 1% of the time, Pallas kernels for 0%

commit v1 on v0

--- a/solution.py
+++ b/solution.py
@@ -95,7 +95,7 @@
     owner_mask = jnp.logical_and(local_latents >= 0, local_latents < dec_rows)
     picked = jnp.take(up_decoder, jnp.clip(local_latents, 0, dec_rows - 1), axis=0)
     picked = picked * owner_mask[:, :, None].astype(jnp.bfloat16)
-    width_full = lax.psum(width_part, "tensor")
+    width_full = jnp.sum(lax.all_gather(width_part, "tensor"), axis=0)
     partial_value = jnp.einsum(
         "ftd,tkd->ftk", width_full, picked.astype(jnp.float32), precision=lax.Precision.HIGHEST
     )

time: 1140 us -> 1320 us (1.16)
  waiting for transfers between devices: 968 us -> 1140 us
    all_gather x0 -> x1, waiting for transfers between devices: none -> 371 us  [on_device(): width_full = jnp.sum(lax.all_gather(width_part, 'tensor'), axis=0)]
    psum x1 -> x0, waiting for transfers between devices: 198 us -> none  [on_device(): width_full = lax.psum(width_part, 'tensor')]
where the time goes in v1:
time: 1320 us
  waiting for transfers between devices  1140 us (86%)
  blocking collectives  99.8 us (8%)
  local copies, waits for them, and re-layouts  32.9 us (2%)
  matrix products  15.8 us (1%)
  other arithmetic  15.1 us (1%)
    unnamed x4, waiting for transfers between devices  490 us
    all_gather x1, waiting for transfers between devices, on_device(): width_full = jnp.sum(lax.all_gather(width_part, 'tensor'), axis=0)  371 us
    psum x1, waiting for transfers between devices, on_device(): lax.psum((gate_part, up_part, neuron_part), ('feature', 'dp'))  283 us
    psum x1, blocking collectives, on_device(): lax.psum(jnp.dot(picker, down_encoder, preferred_element_type=jnp.float32...  99.8 us
  transfers between devices with their start and end apart: 3, of which 3 were waited for; matrix products, arithmetic and copies ran while one was open for 1% of the time, Pallas kernels for 0%

profile of v1, /device:TPU:2, one launch (start us, length us, event | category | flops | bytes accessed | tf_op | source)
XLA Modules:
  0.0 1321.5 jit_solution(11272286426567000991)
XLA Ops:
  6.6 0.8 broadcast_subtract_fusion
  7.4 1.6 fusion.6
  9.0 99.8 %psum.28 = bf16[32,128]{1,0:T(8,128)(2,1)S(1)} all-reduce(f32[32,128]{1,0:T(8,128)S(1)} %fusion.6), channel_id=1, replica_groups=mesh['tensor'=16,'feature'=8,'dp'=4] {'tensor'}, use_global_device_ids=true, to_apply=%region_0.0 | all-reduce | flops 4096 | bytes 24576 | tf_op jit(solution)/shard_map/psum | solution.py:61
  108.8 2.0 fusion.13
  110.8 1.7 fusion.14
  112.5 1.0 convolution_bitcast_fusion
  113.6 283.3 %all-reduce.7.cloned.1.call-done = (f32[4,8,1792]{2,1,0:T(8,128)}, f32[64,1792]{1,0:T(8,128)}, f32[64,1792]{1,0:T(8,128)}) async-done(((f32[4,8,1792]{2,1,0:T(8,128)}, f32[64,1792]{1,0:T(8,128)}, f32[64,1792]{1,0:T(8,128)}), (f32[4,8,1792]{2,1,0:T(8,128)}, f32[64,1792]{1,0:T(8,128)}, f32[64,1792]{1,0:T(8,128)})) %all-reduce.7.cloned.1.call-update) | async-done | bytes 1146896 | tf_op jit(solution)/shard_map/psum | solution.py:68
  396.8 1.4 fusion.7
  398.2 15.8 %while.10 = (s32[]{:T(128)}, f32[4,8,64,128]{3,2,1,0:T(8,128)}, f32[4,8,1792]{2,1,0:T(8,128)}, f32[64,1792]{1,0:T(8,128)S(1)}, bf16[128,1792]{1,0:T(8,128)(2,1)S...) while((s32[]{:T(128)}, f32[4,8,64,128]{3,2,1,0:T(8,128)}, f32[4,8,1792]{2,1,0:T(8,128)}, ...), condition=%wide.region_5.6_spmd, body=%wide.region_4.5_spmd.sunk | while | flops 473497600 | bytes 12493429 | solution.py:92
  398.2 0.8 dynamic-slice_bitcast_fusion.3
  402.2 0.8 dynamic-slice_bitcast_fusion.3
  405.4 0.7 constant_dynamic-update-slice_fusion.2
  406.1 0.8 dynamic-slice_bitcast_fusion.3
  410.1 0.8 dynamic-slice_bitcast_fusion.3
  414.2 12.1 gather_fusion
  426.4 371.0 %all-gather.2.cloned.1.call-done = f32[16,32,64,128]{3,2,1,0:T(8,128)} async-done(((f32[1,32,64,128]{3,2,1,0:T(8,128)}), f32[16,32,64,128]{3,2,1,0:T(8,128)}) %all-gather.2.cloned.1.call-update) | async-done | bytes 16777232 | tf_op jit(solution)/shard_map/all_gather | solution.py:98
  797.4 8.7 reduce_sum.9
  806.1 4.4 convolution_bitcast_fusion.1
  810.5 1.8 copy.15
  812.3 3.2 reshape.35
  815.5 3.4 copy.16
  818.9 4.7 copy.17
  823.6 490.1 %all-reduce.5.cloned.1.call-done = f32[512,4,16,4]{2,3,1,0:T(4,128)} async-done(((f32[512,4,16,4]{2,3,1,0:T(4,128)}), f32[512,4,16,4]{2,3,1,0:T(4,128)}) %all-reduce.5.cloned.1.call-update) | async-done | bytes 524304
  1313.6 1.3 fusion.9
  (43 shorter events, 11.9 us)
Async XLA Ops:
  6.5 407.7 %copy-start = (bf16[8192,128]{1,0:T(8,128)(2,1)S(1)}, bf16[8192,128]{1,0:T(8,128)(2,1)}, u32[]{:S(2)}) copy-start(bf16[8192,128]{1,0:T(8,128)(2,1)} %param.17) | copy-start | bytes 6291460
  6.5 104.3 %copy-start.1 = (bf16[128,1792]{1,0:T(8,128)(2,1)S(1)}, bf16[128,1792]{1,0:T(8,128)(2,1)}, u32[]{:S(2)}) copy-start(bf16[128,1792]{1,0:T(8,128)(2,1)} %param.12) | copy-start | bytes 1376260
  6.5 106.0 %copy-start.3 = (bf16[1792,128]{1,0:T(8,128)(2,1)S(1)}, bf16[1792,128]{1,0:T(8,128)(2,1)}, u32[]{:S(2)}) copy-start(bf16[1792,128]{1,0:T(8,128)(2,1)} %param.14) | copy-start | bytes 1376260
  6.5 390.3 %all-reduce.7.cloned.1.call-start = ((), (), s32[]{:S(2)}) async-start(), calls=%async_computation.2 | async-start | bytes 2293760 | tf_op jit(solution)/shard_map/psum | solution.py:68
  113.5 683.9 %all-gather.2.cloned.1.call-start = ((), (), s32[]{:S(2)}) async-start(), calls=%async_computation | async-start | bytes 17825792 | tf_op jit(solution)/shard_map/all_gather | solution.py:98
  398.2 15.9 %copy-start.4 = (s32[64,64]{1,0:T(8,128)S(1)}, s32[64,64]{1,0:T(8,128)}, u32[]{:S(2)}) copy-start(s32[64,64]{1,0:T(8,128)} %param.18) | copy-start | bytes 49156
  399.8 1.0 copy-start.2
  403.7 1.0 copy-start.2
  407.7 1.0 copy-start.2
  411.6 1.0 copy-start.2
  414.1 899.6 %all-reduce.5.cloned.1.call-start = ((), (), s32[]{:S(2)}) async-start(), calls=%async_computation.1 | async-start | bytes 8388608
  823.5 490.1 %copy-start.5 = (f32[16,4]{0,1:T(4,128)S(1)}, f32[16,4]{0,1:T(4,128)}, u32[]{:S(2)}) copy-start(f32[16,4]{0,1:T(4,128)} %param.19) | copy-start | bytes 772
Sparse Core Ops, SparseCore 0:
  113.6 283.1 all-reduce.6
  414.2 383.1 all-gather.1
  823.7 489.9 all-reduce.4
